TPU v7x, 32 devices: a whole 2x2x4 slice. The times are simulated.
32 devices in a mesh: snp: 2 (over x), rows: 16 (over z, y, core).
Axes of the slice: x: 2, y: 2, z: 4, core: 2. Of those that a mesh axis runs over, the one named last changes fastest.
Arguments:
- genotypes: float32 [3072, 2560], P('snp', 'rows'), may hold values from -1 to 2, as said below
- relationship: float32 [2560, 2560], P('rows', 'snp'), as said below
Outputs:
- updated: float32 [2560, 2560], P('rows', 'snp')
- panel: float32 [2560, 512], P('rows')
Inputs may be any that keep to these rules, and one draw needn't show every extreme that they name: `genotypes`: expected count of the alternative allele, a real number between 0 and 2; exactly -1 marks a missing call. `relationship`: symmetric.
All inputs are finite; a program needn't handle non-finite values.
Results may differ from a plain program's by a relative error of at most 0.0007.
The roundings to bfloat16 on the way count: a program that leaves them out, or rounds other values in their place, can miss the bound.
Values may be sent and summed in bfloat16 or wider, within the bound.
No kernel may reach another device: no remote copies, remote signals or barrier semaphores. Data moves between devices by JAX's collectives and lax.ppermute only.
A program may use at most 128 MiB of HBM per device.

v0:
```python
import jax
import jax.numpy as jnp
from jax import lax
from jax.sharding import PartitionSpec as P

PANEL = 512


RIDGE = 0.25


def from_root(x, axis, root):
    mine = lax.axis_index(axis) == root
    return lax.psum(jnp.where(mine, x, jnp.zeros_like(x)), axis)


def contract_snps(centered, shard_piece):
    return lax.dot_general(
        centered, shard_piece, (((0,), (0,)), ((), ())), preferred_element_type=jnp.float32
    )


def per_device(genotypes, relationship):
    ind_rows = genotypes.shape[1]
    width_cols = relationship.shape[1]
    called = genotypes >= 0
    dosage = jnp.where(called, genotypes, 0.0)
    totals, counts = lax.psum(
        (jnp.sum(dosage, axis=1), jnp.sum(called.astype(jnp.float32), axis=1)), "rows"
    )
    frequency = totals / (2.0 * counts)
    scale_total = lax.psum(jnp.sum(2.0 * frequency * (1.0 - frequency)), "snp")
    centered = jnp.where(called, dosage - 2.0 * frequency[:, None], 0.0).astype(jnp.bfloat16)
    partial_value = contract_snps(centered, lax.all_gather(centered, "rows", axis=1, tiled=True))
    summed = lax.psum_scatter(partial_value, "snp", scatter_dimension=1, tiled=True)
    rank_rows = lax.axis_index("rows")
    rank_snp = lax.axis_index("snp")
    row_ids = rank_rows * ind_rows + lax.broadcasted_iota(jnp.int32, (ind_rows, width_cols), 0)
    col_ids = rank_snp * width_cols + lax.broadcasted_iota(jnp.int32, (ind_rows, width_cols), 1)
    combined = relationship + summed / scale_total
    combined = combined + jnp.where(row_ids == col_ids, RIDGE, 0.0)
    block_count = (PANEL + ind_rows - 1) // ind_rows
    upper_blocks = []
    for root_block in range(block_count):
        upper_blocks.append(from_root(combined, "rows", root_block))
    upper_rows = jnp.concatenate(upper_blocks, axis=0)[:PANEL]
    diag_block, own_columns = (
        from_root(upper_rows[:, :PANEL], "snp", 0),
        from_root(combined[:, :PANEL], "snp", 0),
    )
    factor = jnp.linalg.cholesky(diag_block)
    own_panel = lax.linalg.triangular_solve(
        factor, own_columns, left_side=False, lower=True, transpose_a=True
    )
    column_panel = lax.linalg.triangular_solve(
        factor, upper_rows, left_side=True, lower=True, transpose_a=False
    )
    updated = combined - jnp.dot(own_panel, column_panel, precision=lax.Precision.HIGHEST)
    return (updated, own_panel)


def solution(mesh):
    placed = (P("snp", "rows"), P("rows", "snp"))
    return jax.shard_map(
        per_device,
        mesh=mesh,
        in_specs=placed,
        out_specs=(P("rows", "snp"), P("rows", None)),
        check_vma=False,
    )
```

profile of v0, /device:TPU:0, one launch (start us, length us, event | category | flops | bytes accessed | tf_op | source)
XLA Modules:
  0.0 539.2 jit_solution(10748258667176911262)
XLA Ops:
  8.7 63.0 %all-reduce.1 = (f32[1536]{0:T(1024)S(1)}, f32[1536]{0:T(1024)S(1)}) all-reduce(f32[1536]{0:T(1024)S(1)} %get-tuple-element.17, f32[1536]{0:T(1024)S(1)} %get-tuple-element.16), channel_id=1, replica_groups=mesh['snp'=2,'rows'=16] {'rows'}, use_global_device_ids=true, to_apply=%region_1.2 | all-reduce | flops 3072 | bytes 24576 | tf_op jit(solution)/shard_map/psum | solution.py:28
  73.3 68.9 %all-gather.2.cloned.1.call-done = bf16[1536,2560]{0,1:T(8,128)(2,1)} async-done(((bf16[1536,160]{0,1:T(8,128)(2,1)}), bf16[1536,2560]{0,1:T(8,128)(2,1)}) %all-gather.2.cloned.1.call-update) | async-done | bytes 7864336 | tf_op jit(solution)/shard_map/all_gather | solution.py:34
  142.2 7.2 %fusion.59 = f32[160,2560]{0,1:T(8,128)} fusion(bf16[1536,160]{0,1:T(8,128)(2,1)} %select_convert_fusion, bf16[1536,2560]{0,1:T(8,128)(2,1)} %all-gather.2.cloned.1.call-done), kind=kOutput, calls=%fused_computation.120 | convolution fusion | flops 1258291200 | bytes 9994240 | tf_op jit(solution)/shard_map/dot_general | solution.py:18
  149.5 5.6 %psum.65 = f32[]{:T(128)} all-reduce(f32[]{:T(128)} %get-tuple-element.47), channel_id=1, replica_groups=mesh['snp'=2,'rows'=16] {'snp'}, use_global_device_ids=true, to_apply=%region_6.7 | all-reduce | flops 1 | bytes 8 | tf_op jit(solution)/shard_map/psum | solution.py:32
  155.5 30.0 %reduce-scatter.2.cloned.1.call-done = f32[160,1280]{0,1:T(8,128)} async-done(((f32[160,2560]{0,1:T(8,128)}), f32[160,1280]{0,1:T(8,128)}) %reduce-scatter.2.cloned.1.call-update) | async-done | bytes 819216 | tf_op jit(solution)/shard_map/reduce_scatter | solution.py:35
  185.5 3.3 broadcast_select_fusion.3
  192.0 124.9 %all-reduce.7.cloned.1.call-done = (f32[160,1280]{0,1:T(8,128)}, f32[160,1280]{0,1:T(8,128)}, f32[160,1280]{0,1:T(8,128)}, f32[160,1280]{0,1:T(8,128)}) async-done(((f32[160,1280]{0,1:T(8,128)}, f32[160,1280]{0,1:T(8,128)}, f32[160,1280]{0,1:T(8,128)}, f32[160,1280]{0,1:T(8,128)}), (f32[160,1280]{0,1:T(8,128)}, f32[160,1280]{0,1:T(8,128)}, f32[160,1280]{0,1:T(8,128)}, ...) | async-done | bytes 3276816 | tf_op jit(solution)/shard_map/psum | solution.py:14
  316.9 2.9 fusion.15
  319.9 51.6 %all-reduce.9.cloned.1.call-done = (f32[160,512]{0,1:T(8,128)}, f32[512,512]{0,1:T(8,128)}) async-done(((f32[160,512]{0,1:T(8,128)}, f32[512,512]{0,1:T(8,128)}), (f32[160,512]{0,1:T(8,128)}, f32[512,512]{0,1:T(8,128)})) %all-reduce.9.cloned.1.call-update) | async-done | bytes 1376272 | tf_op jit(solution)/shard_map/psum | solution.py:14
  373.4 11.7 %cholesky.103 = f32[128,128]{1,0:T(8,128)S(1)} custom-call(f32[128,128]{1,0:T(8,128)S(1)} %cholesky.263), custom_call_target="Cholesky" | custom-call | tf_op jit(solution)/shard_map/jit(cholesky)/cholesky | solution.py:51
  385.2 9.8 %custom-call.32 = f32[1,128,128]{1,2,0:T(8,128)S(1)} custom-call(f32[1,128,128]{2,1,0:T(8,128)S(1)} %get-tuple-element.46), custom_call_target="InvertDiagBlocksLowerTriangular" | custom-call | tf_op jit(solution)/shard_map/jit(cholesky)/cholesky | solution.py:51
  395.7 11.7 %cholesky.215 = f32[128,128]{1,0:T(8,128)S(1)} custom-call(f32[128,128]{1,0:T(8,128)S(1)} %cholesky.267), custom_call_target="Cholesky" | custom-call | tf_op jit(solution)/shard_map/jit(cholesky)/cholesky | solution.py:51
  407.7 10.2 %custom-call.33 = f32[1,128,128]{1,2,0:T(8,128)S(1)} custom-call(f32[1,128,128]{2,1,0:T(8,128)S(1)} %get-tuple-element.44), custom_call_target="InvertDiagBlocksLowerTriangular" | custom-call | tf_op jit(solution)/shard_map/jit(cholesky)/cholesky | solution.py:51
  419.0 11.7 %cholesky.236 = f32[128,128]{1,0:T(8,128)S(1)} custom-call(f32[128,128]{1,0:T(8,128)S(1)} %cholesky.272), custom_call_target="Cholesky" | custom-call | tf_op jit(solution)/shard_map/jit(cholesky)/cholesky | solution.py:51
  430.9 9.8 %custom-call.34 = f32[1,128,128]{1,2,0:T(8,128)S(1)} custom-call(f32[1,128,128]{2,1,0:T(8,128)S(1)} %get-tuple-element.42), custom_call_target="InvertDiagBlocksLowerTriangular" | custom-call | tf_op jit(solution)/shard_map/jit(cholesky)/cholesky | solution.py:51
  441.5 11.9 %cholesky.253 = f32[128,128]{1,0:T(8,128)S(1)} custom-call(f32[128,128]{1,0:T(8,128)S(1)} %convolution_subtract_fusion.9), custom_call_target="Cholesky" | custom-call | tf_op jit(solution)/shard_map/jit(cholesky)/cholesky | solution.py:51
  459.2 12.4 %while.1 = (s32[]{:T(128)}, f32[512,512]{0,1:T(8,128)}, s32[4,2]{0,1:T(2,128)S(1)}, f32[4,128,128]{2,1,0:T(8,128)S(1)}, s32[]{:T(128)}) while((s32[]{:T(128)}, f32[512,512]{0,1:T(8,128)}, s32[4,2]{0,1:T(2,128)S(1)}, f32[4,128,128]{2,1,0:T(8,128)S(1)}, s32[]{:T(128)}) %tuple.34), condition=%wide.while_cond, body=%wide.while_body.sunk | while | flops 2 | bytes 393321 | solution.py:52
  459.8 2.3 dynamic-slice.7
  462.9 2.3 dynamic-slice.7
  466.1 2.3 dynamic-slice.7
  471.6 39.3 %custom-call.35 = f32[4,128,128]{1,2,0:T(8,128)S(1)} custom-call(f32[4,128,128]{2,1,0:T(8,128)S(1)} %get-tuple-element.9), custom_call_target="InvertDiagBlocksLowerTriangular" | custom-call | tf_op jit(solution)/shard_map/triangular_solve | solution.py:52
  515.2 2.5 convolution_subtract_fusion.2
  519.0 3.6 convolution_subtract_fusion.1
  526.7 4.4 convolution_subtract_fusion
  (103 shorter events, 31.0 us)
Async XLA Ops:
  7.2 65.1 %copy-start.8 = (f32[1536,160]{0,1:T(8,128)S(1)}, f32[1536,160]{0,1:T(8,128)}, u32[]{:S(2)}) copy-start(f32[1536,160]{0,1:T(8,128)} %param.2) | copy-start | bytes 2949124
  7.2 135.0 %all-gather.2.cloned.1.call-start = ((), (), s32[]{:S(2)}) async-start(), calls=%async_computation.1 | async-start | bytes 8355840 | tf_op jit(solution)/shard_map/all_gather | solution.py:34
  73.2 112.3 %reduce-scatter.2.cloned.1.call-start = ((), (), s32[]{:S(2)}) async-start(), calls=%async_computation.2 | async-start | bytes 3932160 | tf_op jit(solution)/shard_map/reduce_scatter | solution.py:35
  149.4 5.7 %copy-start.9 = (f32[160,1280]{1,0:T(8,128)S(1)}, f32[160,1280]{1,0:T(8,128)}, u32[]{:S(2)}) copy-start(f32[160,1280]{1,0:T(8,128)} %param.3) | copy-start | bytes 2457604
  149.4 167.5 %all-reduce.7.cloned.1.call-start = ((), (), s32[]{:S(2)}) async-start(), calls=%async_computation.3 | async-start | bytes 10485760 | tf_op jit(solution)/shard_map/psum | solution.py:14
  188.8 2.3 copy-start.3
  190.9 180.6 %all-reduce.9.cloned.1.call-start = ((), (), s32[]{:S(2)}) async-start(), calls=%async_computation.4 | async-start | bytes 3145728 | tf_op jit(solution)/shard_map/psum | solution.py:14
  371.5 1.7 copy-start.7
  458.0 52.9 %copy-start.2 = (f32[160,1280]{0,1:T(8,128)S(1)}, f32[160,1280]{0,1:T(8,128)}, u32[]{:S(2)}) copy-start(f32[160,1280]{0,1:T(8,128)} %get-tuple-element.31) | copy-start | bytes 2457604
  459.2 52.5 %copy-start = (f32[160,1280]{0,1:T(8,128)S(1)}, f32[160,1280]{0,1:T(8,128)}, u32[]{:S(2)}) copy-start(f32[160,1280]{0,1:T(8,128)} %get-tuple-element.30) | copy-start | bytes 2457604
  511.7 3.0 copy-start.6
  513.9 1.3 copy-start.1
  517.7 1.3 copy-start.5
  522.6 1.0 copy-start.10
  524.4 2.3 copy-start.4
  526.7 4.5 copy-start.11
Sparse Core Ops, SparseCore 0:
  73.3 68.8 all-gather.1
  149.5 35.8 reduce-scatter.1
  191.0 125.8 all-reduce.6
  320.0 51.4 all-reduce.8
where the time goes:
time: 543 us; the launch traced here: 539 us
  waiting for transfers between devices  276 us (51%)
  other arithmetic  132 us (24%)
  blocking collectives  68.5 us (13%)
  matrix products  28.2 us (5%)
  local copies, waits for them, and re-layouts  17.6 us (3%)
  between operations  17 us (3%)
    psum x2, waiting for transfers between devices, from_root(): return lax.psum(jnp.where(mine, x, jnp.zeros_like(x)), axis)  177 us
    another operation x14, other arithmetic, per_device(): factor = jnp.linalg.cholesky(diag_block)  79 us
    all_gather x1, waiting for transfers between devices, per_device(): lax.all_gather(centered, 'rows', axis=1, tiled=True)  68.9 us
    psum x1, blocking collectives, per_device(): lax.psum((jnp.sum(dosage, axis=1), jnp.sum(called.astype(jnp.float32), ax...  63 us
    another operation x4, other arithmetic, per_device(): lax.linalg.triangular_solve(factor, own_columns, left_side=False, lower=T...  40.5 us
    reduce_scatter x1, waiting for transfers between devices, per_device(): lax.psum_scatter(partial_value, 'snp', scatter_dimension=1, tiled=True)  30 us
    another operation x20, local copies, waits for them, and re-layouts  12.3 us
    another operation x7, matrix products, per_device(): lax.linalg.triangular_solve(factor, upper_rows, left_side=True, lower=Tru...  11.3 us
  transfers between devices with their start and end apart: 4, of which 4 were waited for; matrix products, arithmetic and copies ran while one was open for 0% of the time, Pallas kernels for 0%

commit v1 on v0

v1 whole, which is shorter than its diff:
```python
import jax
import jax.numpy as jnp
from jax import lax
from jax.experimental import pallas as pl
from jax.experimental.pallas import tpu as pltpu
from jax.sharding import PartitionSpec as P

PANEL = 512
RIDGE = 0.25
GROUP = 4


BLOCK = 128
SUB = 8


def factor_kernel(a_ref, out_ref, work):
    work[...] = a_ref[...]
    lane = lax.broadcasted_iota(jnp.int32, (SUB, BLOCK), 1)
    for g in range(BLOCK // SUB):
        at = g * SUB
        own = work[at : at + SUB, :]
        inside = (lane >= at) & (lane < at + SUB)
        rows = [jnp.broadcast_to(own[u : u + 1, :], (SUB, BLOCK)) for u in range(SUB)]
        e = [
            [
                jnp.broadcast_to(rows[t][:, at + u : at + u + 1], (SUB, BLOCK))
                for t in range(u + 1)
            ]
            for u in range(SUB)
        ]
        rows = [
            jnp.where(inside, jnp.where(lane == at + u, 1.0, 0.0), rows[u])
            for u in range(SUB)
        ]
        low = [[None] * SUB for _ in range(SUB)]
        scale = []
        for t in range(SUB):
            r = lax.rsqrt(e[t][t])
            scale.append(r)
            for u in range(t + 1, SUB):
                low[u][t] = e[u][t] * r
            for u in range(t + 1, SUB):
                for v in range(t + 1, u + 1):
                    e[u][v] = e[u][v] - low[u][t] * low[v][t]
            rows[t] = rows[t] * r
            for u in range(t + 1, SUB):
                rows[u] = rows[u] - low[u][t] * rows[t]
        for below in range(g + 1, BLOCK // SUB):
            base = below * SUB
            rest = work[base : base + SUB, :]
            c = [
                jnp.broadcast_to(rest[:, at + t : at + t + 1], (SUB, BLOCK))
                for t in range(SUB)
            ]
            rest = jnp.where(inside, 0.0, rest)
            for t in range(SUB):
                c[t] = c[t] * scale[t]
                for s in range(t + 1, SUB):
                    c[s] = c[s] - low[s][t] * c[t]
                rest = rest - c[t] * rows[t]
            work[base : base + SUB, :] = rest
        for t in range(SUB):
            work[at + t : at + t + 1, :] = rows[t][0:1, :]
    i = lax.broadcasted_iota(jnp.int32, (BLOCK, BLOCK), 0)
    j = lax.broadcasted_iota(jnp.int32, (BLOCK, BLOCK), 1)
    out_ref[...] = jnp.where(j <= i, work[...], 0.0)


def factor_inverse(a):
    return pl.pallas_call(
        factor_kernel,
        out_shape=jax.ShapeDtypeStruct((BLOCK, BLOCK), jnp.float32),
        in_specs=[pl.BlockSpec(memory_space=pltpu.VMEM)],
        out_specs=pl.BlockSpec(memory_space=pltpu.VMEM),
        scratch_shapes=[pltpu.VMEM((BLOCK, BLOCK), jnp.float32)],
        cost_estimate=pl.CostEstimate(flops=4_000_000_000, bytes_accessed=131072, transcendentals=128),
    )(a)


def precise(a, b, contract):
    return lax.dot_general(
        a,
        b,
        (((1,), (contract,)), ((), ())),
        precision=lax.Precision.HIGHEST,
        preferred_element_type=jnp.float32,
    )


def solve_panel(diag_block, own_columns):
    blocks = PANEL // BLOCK
    rest = jnp.concatenate([diag_block, own_columns], axis=0)
    inverses, columns = [], []
    for k in range(blocks):
        inverse = factor_inverse(rest[:BLOCK, :BLOCK])
        column = precise(rest[BLOCK:, :BLOCK], inverse, 1)
        inverses.append(inverse)
        columns.append(column)
        if k + 1 < blocks:
            left = (blocks - 1 - k) * BLOCK
            rest = rest[BLOCK:, BLOCK:] - precise(column, column[:left], 1)
    own = own_columns.shape[0]
    panel = [c[-own:] for c in columns]
    weights = [None] * blocks
    for k in reversed(range(blocks)):
        total = panel[k]
        for j in range(k + 1, blocks):
            start = (j - k - 1) * BLOCK
            total = total - precise(weights[j], columns[k][start : start + BLOCK], 0)
        weights[k] = precise(total, inverses[k], 0)
    return jnp.concatenate(panel, axis=1), jnp.concatenate(weights, axis=1)


def select_order(blocks, q):
    low = (q & 1) == 1
    high = (q & 2) == 2
    b = [
        jnp.where(low, blocks[k ^ 1], blocks[k]) for k in range(GROUP)
    ]
    return [jnp.where(high, b[k ^ 2], b[k]) for k in range(GROUP)]


def make(n_rows, n_snp):
    lines = n_rows // GROUP

    def rows_xor(x, bits):
        return lax.ppermute(x, "rows", [(r, r ^ bits) for r in range(n_rows)])

    def line_next(x):
        return lax.ppermute(
            x, "rows", [(r, (r + GROUP) % n_rows) for r in range(n_rows)]
        )

    def snp_xor(x, bits):
        return lax.ppermute(x, "snp", [(s, s ^ bits) for s in range(n_snp)])

    def from_first_snp(x, rank):
        got = x
        for s in range(1, n_snp):
            moved = lax.ppermute(x, "snp", [(0, s)])
            got = jnp.where(rank == s, moved, got)
        return got

    def group_gather(x):
        core = rows_xor(x, 1)
        other = rows_xor(x, 2)
        return [x, core, other, rows_xor(other, 1)]

    def rows_sum(x):
        bit = 1
        while bit < n_rows:
            if bit * 2 < n_rows:
                parts = [x] + [rows_xor(x, bit * k) for k in (1, 2, 3)]
                x = (parts[0] + parts[1]) + (parts[2] + parts[3])
                bit *= 4
            else:
                x = x + rows_xor(x, bit)
                bit *= 2
        return x

    def snp_sum(x):
        bit = 1
        while bit < n_snp:
            x = x + snp_xor(x, bit)
            bit *= 2
        return x

    def times(a, b):
        return lax.dot_general(
            a, b, (((1,), (1,)), ((), ())), preferred_element_type=jnp.float32
        )

    def per_device(genotypes, relationship):
        snps, own = genotypes.shape
        width = relationship.shape[1]
        rank = lax.axis_index("rows")
        col = lax.axis_index("snp")
        q = rank % GROUP
        z = rank // GROUP
        part = lines // n_snp

        rel_own = from_first_snp(relationship[:, :PANEL], col)
        rel_ring = [rel_own]
        for _ in range(lines - 1):
            rel_ring.append(line_next(rel_ring[-1]))

        called = genotypes >= 0
        dosage = jnp.where(called, genotypes, 0.0)
        stats = jnp.stack(
            [jnp.sum(dosage, axis=1), jnp.sum(called.astype(jnp.float32), axis=1)]
        )
        stats = rows_sum(stats)
        frequency = stats[0] / (2.0 * stats[1])
        scale_total = snp_sum(jnp.sum(2.0 * frequency * (1.0 - frequency)).reshape(1, 1))
        inverse = (1.0 / scale_total)[0, 0]
        gt = genotypes.T
        centered = jnp.where(gt >= 0, gt - 2.0 * frequency[None, :], 0.0).astype(
            jnp.bfloat16
        )

        ring = [centered]
        for _ in range(lines - 1):
            ring.append(line_next(ring[-1]))
        line = jnp.stack(ring)
        rel_line = jnp.stack(rel_ring)

        def of_line(stack, target):
            return lax.dynamic_index_in_dim(
                stack, jnp.mod(z - target, lines), 0, keepdims=False
            )

        first = of_line(line, 0)
        head = jnp.concatenate(select_order(group_gather(first), q), axis=0)[:PANEL]
        plane = jnp.concatenate(group_gather(centered), axis=0)

        lead = snp_sum(times(jnp.concatenate([first, centered], axis=0), head))
        rel_lead = jnp.concatenate([of_line(rel_line, 0), rel_own], axis=0)
        lead = rel_lead + lead * inverse
        eye_rows = lax.broadcasted_iota(jnp.int32, lead.shape, 0)
        eye_cols = lax.broadcasted_iota(jnp.int32, lead.shape, 1)
        ids = jnp.where(eye_rows < own, q * own + eye_rows, (rank - 1) * own + eye_rows)
        lead = lead + jnp.where(ids == eye_cols, RIDGE, 0.0)
        own_columns = lead[own:]
        diag_block = jnp.concatenate(
            select_order(group_gather(lead[:own]), q), axis=0
        )[:PANEL]

        mine = None
        for bits in range(n_snp):
            target = col ^ bits
            cols = jnp.concatenate(
                [of_line(line, target * part + j) for j in range(part)], axis=0
            )
            gram = times(plane, cols)
            side = times(cols, head)
            if bits:
                gram, side = snp_xor(gram, bits), snp_xor(side, bits)
                mine = (mine[0] + gram, mine[1] + side)
            else:
                mine = (gram, side)
        gram, side = mine
        rel_side = jnp.concatenate(
            [of_line(rel_line, col * part + j) for j in range(part)], axis=0
        )
        side = rel_side + side * inverse
        side_rows = lax.broadcasted_iota(jnp.int32, side.shape, 0)
        side_ids = (
            (col * part + side_rows // own) * GROUP + q
        ) * own + side_rows % own
        side = side + jnp.where(
            side_ids == lax.broadcasted_iota(jnp.int32, side.shape, 1), RIDGE, 0.0
        )
        side = select_order(group_gather(side), q)
        side = jnp.stack([s.reshape(part, own, PANEL) for s in side], axis=1)
        side = side.reshape(width, PANEL)

        gram = gram.reshape(GROUP, own, part * own)
        pieces = [gram[0]] + [rows_xor(gram[k], k) for k in range(1, GROUP)]
        pieces = select_order(pieces, q)
        summed = jnp.stack([p.reshape(own, part, own) for p in pieces], axis=2)
        summed = summed.reshape(own, width)
        row_ids = rank * own + lax.broadcasted_iota(jnp.int32, (own, width), 0)
        col_ids = col * width + lax.broadcasted_iota(jnp.int32, (own, width), 1)
        combined = relationship + summed * inverse
        combined = combined + jnp.where(row_ids == col_ids, RIDGE, 0.0)

        panel, weights = solve_panel(diag_block, own_columns)
        updated = combined - precise(weights, side, 1)
        return updated, panel

    return per_device


def solution(mesh):
    return jax.shard_map(
        make(mesh.shape["rows"], mesh.shape["snp"]),
        mesh=mesh,
        in_specs=(P("snp", "rows"), P("rows", "snp")),
        out_specs=(P("rows", "snp"), P("rows", None)),
        check_vma=False,
    )
```

time: 543 us -> 195 us (0.36)
  waiting for transfers between devices: 276 us -> 104 us
  other arithmetic: 132 us -> 11.6 us
  blocking collectives: 68.5 us -> 0 us
  Pallas kernels: 0 us -> 22.1 us
  starting transfers between devices: 0.34 us -> 22.3 us
  between operations: 17 us -> 2.6 us
  local copies, waits for them, and re-layouts: 17.6 us -> 9.41 us
  matrix products: 28.2 us -> 20.7 us
    psum x2 -> x0, waiting for transfers between devices: 177 us -> none  [from_root(): return lax.psum(jnp.where(mine, x, jnp.zeros_like(x)), axis)]
    another operation x18 -> x5, other arithmetic: 119 us -> 2.69 us  [the longest x2 2.34 us: per_device(): line = jnp.stack(ring)]
    ppermute x0 -> x32, waiting for transfers between devices: none -> 104 us  [the longest x6 51 us: line_next(): lax.ppermute(x, 'rows', [(r, (r + GROUP) % n_rows) for r in range(n_rows)])]
    all_gather x1 -> x0, waiting for transfers between devices: 68.9 us -> none  [per_device(): lax.all_gather(centered, 'rows', axis=1, tiled=True)]
    psum x2 -> x0, blocking collectives: 68.5 us -> none  [the longest x1 63 us: per_device(): lax.psum((jnp.sum(dosage, axis=1), jnp.sum(called.astype(jnp.float32), ax...]
    reduce_scatter x1 -> x0, waiting for transfers between devices: 30 us -> none  [per_device(): lax.psum_scatter(partial_value, 'snp', scatter_dimension=1, tiled=True)]
    ppermute x0 -> x32, starting transfers between devices: none -> 22.3 us  [the longest x21 13.5 us: rows_xor(): return lax.ppermute(x, 'rows', [(r, r ^ bits) for r in range(n_rows)])]
    pallas_call x0 -> x4, Pallas kernels: none -> 22.1 us  [factor_inverse(): pl.pallas_call(factor_kernel, out_shape=jax.ShapeDtypeStruct((BLOCK, BLOC...]
  transfers between devices with their start and end apart: 4 -> 32, of which waited for: 4 -> 14; matrix products, arithmetic and copies ran while one was open for 0% -> 15% of each run, Pallas kernels for 0% -> 11%
where the time goes in v1:
time: 195 us; the launch traced here: 193 us
  waiting for transfers between devices  104 us (53%)
  starting transfers between devices  22.3 us (11%)
  Pallas kernels  22.1 us (11%)
  matrix products  20.7 us (11%)
  other arithmetic  11.6 us (6%)
  local copies, waits for them, and re-layouts  9.41 us (5%)
  between operations  2.6 us (1%)
    ppermute x6, waiting for transfers between devices, line_next(): lax.ppermute(x, 'rows', [(r, (r + GROUP) % n_rows) for r in range(n_rows)])  51 us
    ppermute x4, waiting for transfers between devices, snp_xor(): return lax.ppermute(x, 'snp', [(s, s ^ bits) for s in range(n_snp)])  34.5 us
    pallas_call x4, Pallas kernels, factor_inverse(): pl.pallas_call(factor_kernel, out_shape=jax.ShapeDtypeStruct((BLOCK, BLOC...  22.1 us
    ppermute x21, waiting for transfers between devices, rows_xor(): return lax.ppermute(x, 'rows', [(r, r ^ bits) for r in range(n_rows)])  18.3 us
    ppermute x21, starting transfers between devices, rows_xor(): return lax.ppermute(x, 'rows', [(r, r ^ bits) for r in range(n_rows)])  13.5 us
    dot_general x18, matrix products, precise(): lax.dot_general(a, b, (((1,), (contract,)), ((), ())), precision=lax.Prec...  12.3 us
    dot_general x5, matrix products, times(): lax.dot_general(a, b, (((1,), (1,)), ((), ())), preferred_element_type=jn...  8.38 us
    select_n x4, other arithmetic, select_order(): return [jnp.where(high, b[k ^ 2], b[k]) for k in range(GROUP)]  5.47 us
  transfers between devices with their start and end apart: 32, of which 14 were waited for; matrix products, arithmetic and copies ran while one was open for 15% of the time, Pallas kernels for 11%

profile of v1, /device:TPU:0, one launch (start us, length us, event | category | flops | bytes accessed | tf_op | source)
XLA Modules:
  0.0 192.6 jit_solution(1410846969204449637)
XLA Ops:
  2.7 2.6 %collective-permute-start.1 = (f32[2,1536]{1,0:T(2,128)S(1)}, f32[2,1536]{1,0:T(2,128)S(1)}, u32[]{:S(2)}, u32[]{:S(2)}) collective-permute-start(f32[2,1536]{1,0:T(2,128)S(1)} %pad_maximum_fusion.18), channel_id=1, source_target_pairs={{0,2},{1,3},{2,0},{3,1},{4,6},{5,7},{6,4},{7,5},{8,10},{9,11},{10,... | collective-permute-start | bytes 36872 | tf_op jit(solution)/shard_map/ppermute | solution.py:128
  10.1 2.6 %collective-permute-start.4 = (f32[2,1536]{1,0:T(2,128)S(1)}, f32[2,1536]{1,0:T(2,128)S(1)}, u32[]{:S(2)}, u32[]{:S(2)}) collective-permute-start(f32[2,1536]{1,0:T(2,128)S(1)} %add_add_fusion.1), channel_id=1, source_target_pairs={{0,8},{1,9},{2,10},{3,11},{4,12},{5,13},{6,14},{7,15},{8,0},{9,1},... | collective-permute-start | bytes 36872 | tf_op jit(solution)/shard_map/ppermute | solution.py:128
  14.7 3.5 %collective-permute-done.5 = f32[2,1536]{1,0:T(2,128)S(1)} collective-permute-done((f32[2,1536]{1,0:T(2,128)S(1)}, f32[2,1536]{1,0:T(2,128)S(1)}, u32[]{:S(2)}, u32[]{:S(2)}) %collective-permute-start.5) | collective-permute-done | bytes 12320 | tf_op jit(solution)/shard_map/ppermute | solution.py:128
  18.8 2.1 %fusion.31 = (bf16[1,160,1536]{2,1,0:T(8,128)(2,1)S(1)}, bf16[160,1536]{1,0:T(8,128)(2,1)}) fusion(f32[1536,160]{0,1:T(8,128)} %param.2, f32[1536]{0:T(1024)S(1)} %get-tuple-element.5), kind=kLoop, calls=%fused_computation.104 | loop fusion | flops 983040 | bytes 1972224 | tf_op jit(solution)/shard_map/stack | solution.py:205
  20.9 13.6 %collective-permute-done.9 = bf16[160,1536]{1,0:T(8,128)(2,1)S(1)} collective-permute-done((bf16[160,1536]{1,0:T(8,128)(2,1)}, bf16[160,1536]{1,0:T(8,128)(2,1)S(1)}, u32[]{:S(2)}, u32[]{:S(2)}) %collective-permute-start.9) | collective-permute-done | bytes 491552 | tf_op jit(solution)/shard_map/ppermute | solution.py:131
  34.5 3.4 %collective-permute-start.17 = (f32[160,512]{1,0:T(8,128)S(1)}, f32[160,512]{1,0:T(8,128)S(1)}, u32[]{:S(2)}, u32[]{:S(2)}) collective-permute-start(f32[160,512]{1,0:T(8,128)S(1)} %slice.112), channel_id=1, source_target_pairs={{0,16},{1,17},{2,18},{3,19},{4,20},{5,21},{6,22},{7,23},{8,24},{9,... | collective-permute-start | bytes 983048 | tf_op jit(solution)/shard_map/ppermute | solution.py:141
  37.9 9.0 %collective-permute-done.10 = bf16[160,1536]{1,0:T(8,128)(2,1)S(1)} collective-permute-done((bf16[160,1536]{1,0:T(8,128)(2,1)S(1)}, bf16[160,1536]{1,0:T(8,128)(2,1)S(1)}, u32[]{:S(2)}, u32[]{:S(2)}) %collective-permute-start.10) | collective-permute-done | bytes 491552 | tf_op jit(solution)/shard_map/ppermute | solution.py:131
  47.8 17.7 %collective-permute-done.18 = f32[160,512]{1,0:T(8,128)S(1)} collective-permute-done((f32[160,512]{1,0:T(8,128)S(1)}, f32[160,512]{1,0:T(8,128)S(1)}, u32[]{:S(2)}, u32[]{:S(2)}) %collective-permute-start.18) | collective-permute-done | bytes 327712 | tf_op jit(solution)/shard_map/ppermute | solution.py:131
  67.3 8.1 %collective-permute-done.19 = f32[160,512]{1,0:T(8,128)S(1)} collective-permute-done((f32[160,512]{1,0:T(8,128)S(1)}, f32[160,512]{1,0:T(8,128)S(1)}, u32[]{:S(2)}, u32[]{:S(2)}) %collective-permute-start.19) | collective-permute-done | bytes 327712 | tf_op jit(solution)/shard_map/ppermute | solution.py:131
  77.5 2.1 %collective-permute-done.16 = f32[1,1]{1,0:T(1,128)} collective-permute-done((f32[1,1]{1,0:T(1,128)}, f32[1,1]{1,0:T(1,128)}, u32[]{:S(2)}, u32[]{:S(2)}) %collective-permute-start.16) | collective-permute-done | bytes 36 | tf_op jit(solution)/shard_map/ppermute | solution.py:136
  81.6 2.6 %collective-permute-done.20 = f32[160,512]{1,0:T(8,128)S(1)} collective-permute-done((f32[160,512]{1,0:T(8,128)S(1)}, f32[160,512]{1,0:T(8,128)S(1)}, u32[]{:S(2)}, u32[]{:S(2)}) %collective-permute-start.20) | collective-permute-done | bytes 327712 | tf_op jit(solution)/shard_map/ppermute | solution.py:131
  85.3 2.1 %fusion.10 = f32[640,320]{0,1:T(8,128)S(1)} fusion(bf16[160,1536]{1,0:T(8,128)(2,1)S(1)} %get-tuple-element.12, bf16[160,1536]{1,0:T(8,128)(2,1)S(1)} %copy-done.7, bf16[160,1536]{1,0:T(8,128)(2,1)S(1)} %collective-permute-done.8, bf16[160,1536]{1,0:T(8,128)(2,1)} %collective-permute-done.7, bf16[160,1536]{1,0:T(8,128)(2,1)S(1)} %collective-permute-done.6, ...), kind=kOutput, calls=%fused_computation.42 | convolution fusion | flops 638976000 | bytes 3768320 | tf_op jit(solution)/shard_map/dot_general | solution.py:170
  94.8 13.8 %collective-permute-done.12 = f32[640,320]{0,1:T(8,128)S(1)} collective-permute-done((f32[640,320]{0,1:T(8,128)S(1)}, f32[640,320]{0,1:T(8,128)S(1)}, u32[]{:S(2)}, u32[]{:S(2)}) %collective-permute-start.12) | collective-permute-done | bytes 819232 | tf_op jit(solution)/shard_map/ppermute | solution.py:136
  108.7 2.2 %convolution_add_fusion = f32[640,320]{0,1:T(8,128)S(1)} fusion(f32[640,320]{0,1:T(8,128)S(1)} %collective-permute-done.12, bf16[160,1536]{1,0:T(8,128)(2,1)S(1)} %get-tuple-element.14, bf16[160,1536]{1,0:T(8,128)(2,1)S(1)} %get-tuple-element.10, bf16[160,1536]{1,0:T(8,128)(2,1)S(1)} %collective-permute-done.8, ...), kind=kOutput, calls=%fused_computation.14 | convolution fusion | flops 639180800 | bytes 4587520 | tf_op jit(solution)/shard_map/dot_general | solution.py:170
  113.1 9.6 %collective-permute-done.24 = f32[320,512]{1,0:T(8,128)S(1)} collective-permute-done((f32[320,512]{1,0:T(8,128)S(1)}, f32[320,512]{1,0:T(8,128)S(1)}, u32[]{:S(2)}, u32[]{:S(2)}) %collective-permute-start.24) | collective-permute-done | bytes 655392 | tf_op jit(solution)/shard_map/ppermute | solution.py:136
  124.2 9.0 %collective-permute-done.28 = f32[320,512]{1,0:T(8,128)S(1)} collective-permute-done((f32[320,512]{1,0:T(8,128)S(1)}, f32[320,512]{1,0:T(8,128)S(1)}, u32[]{:S(2)}, u32[]{:S(2)}) %collective-permute-start.28) | collective-permute-done | bytes 655392 | tf_op jit(solution)/shard_map/ppermute | solution.py:136
  138.5 10.0 %collective-permute-done.29 = f32[320,512]{1,0:T(8,128)} collective-permute-done((f32[320,512]{1,0:T(8,128)}, f32[320,512]{1,0:T(8,128)}, u32[]{:S(2)}, u32[]{:S(2)}) %collective-permute-start.29) | collective-permute-done | bytes 655392 | tf_op jit(solution)/shard_map/ppermute | solution.py:128
  148.5 2.1 %broadcast_select_fusion.24 = (f32[160,512]{1,0:T(8,128)S(1)}, f32[160,512]{1,0:T(8,128)S(1)}, f32[160,512]{1,0:T(8,128)S(1)}, f32[160,512]{1,0:T(8,128)S(1)}, f32[160,512]{1,0:T(8,128)}) fusion(pred[]{:T(512)S(6)} %eq.36, f32[160,512]{1,0:T(8,128)} %collective-permute-done.26, f32[160,512]{1,0:T(8,128)} %collective-permute-done.25, pred[]{:T(512)S(6)} %eq.37, ...), kind=kLoop, calls=%fused_computation.92 | loop fusion | flops 655360 | bytes 3276802 | tf_op jit(solution)/shard_map/jit(_where)/select_n | solution.py:121
  151.2 5.5 %shard_map.41 = f32[128,128]{1,0:T(8,128)} custom-call(f32[128,128]{1,0:T(8,128)} %slice.148.a_ref), custom_call_target="tpu_custom_call" | custom-call | flops 4000000000 | bytes 131072 | tf_op jit(solution)/shard_map/pallas_call | solution.py:71
  159.5 5.5 %shard_map.42 = f32[128,128]{1,0:T(8,128)} custom-call(f32[128,128]{1,0:T(8,128)} %slice.153.a_ref), custom_call_target="tpu_custom_call" | custom-call | flops 4000000000 | bytes 131072 | tf_op jit(solution)/shard_map/pallas_call | solution.py:71
  167.3 5.7 %shard_map.43 = f32[128,128]{1,0:T(8,128)} custom-call(f32[128,128]{1,0:T(8,128)} %slice.158.a_ref), custom_call_target="tpu_custom_call" | custom-call | flops 4000000000 | bytes 131072 | tf_op jit(solution)/shard_map/pallas_call | solution.py:71
  175.1 5.5 %shard_map.44 = f32[128,128]{1,0:T(8,128)} custom-call(f32[128,128]{1,0:T(8,128)} %slice.163.a_ref), custom_call_target="tpu_custom_call" | custom-call | flops 4000000000 | bytes 131072 | tf_op jit(solution)/shard_map/pallas_call | solution.py:71
  185.5 2.0 %broadcast_select_fusion.15 = (f32[320,512]{1,0:T(8,128)S(1)}, f32[320,512]{1,0:T(8,128)S(1)}, f32[320,512]{1,0:T(8,128)S(1)}, f32[320,512]{1,0:T(8,128)S(1)}) fusion(pred[]{:T(512)S(6)} %eq.36, f32[320,512]{1,0:T(8,128)} %collective-permute-done.30, f32[320,512]{1,0:T(8,128)} %collective-permute-done.29, pred[]{:T(512)S(6)} %eq.37, ...), kind=kLoop, calls=%fused_computation.75 | loop fusion | flops 1310720 | bytes 5242882 | tf_op jit(solution)/shard_map/jit(_where)/select_n | solution.py:121
  188.7 3.8 %convolution_subtract_fusion = f32[160,1280]{1,0:T(8,128)} fusion(f32[1280,512]{1,0:T(8,128)S(1)} %bitcast.69, f32[160,1280]{1,0:T(8,128)S(1)} %copy-done.1, f32[160,1280]{1,0:T(8,128)S(1)} %mul.75, s32[1280]{0:T(1024)S(1)} %iota_add_fusion, s32[160]{0:T(256)S(1)} %iota_add_fusion.3, f32[160,128]{1,0:T(8,128)S(1)} %fusion.54, f32[160,128]{1,0:T(8,128)S(1)} %fusion.55, ...), kind=kOutput, calls=%fused_computation.1 | convolution fusion | flops 1259560960 | bytes 5412480 | tf_op jit(solution)/shard_map/dot_general | solution.py:82
  (131 shorter events, 45.9 us)
Async XLA Ops:
  20.9 13.6 %collective-permute-start.9 = (bf16[160,1536]{1,0:T(8,128)(2,1)}, bf16[160,1536]{1,0:T(8,128)(2,1)S(1)}, u32[]{:S(2)}, u32[]{:S(2)}) collective-permute-start(bf16[160,1536]{1,0:T(8,128)(2,1)} %get-tuple-element.31), channel_id=1, source_target_pairs={{0,4},{1,5},{2,6},{3,7},{4,8},{5,9},{6,10},{7,11},{8,12},{9,13},{1... | collective-permute-start | bytes 1474568 | tf_op jit(solution)/shard_map/ppermute | solution.py:131
  34.5 12.5 %collective-permute-start.10 = (bf16[160,1536]{1,0:T(8,128)(2,1)S(1)}, bf16[160,1536]{1,0:T(8,128)(2,1)S(1)}, u32[]{:S(2)}, u32[]{:S(2)}) collective-permute-start(bf16[160,1536]{1,0:T(8,128)(2,1)S(1)} %collective-permute-done.9), channel_id=1, source_target_pairs={{0,4},{1,5},{2,6},{3,7},{4,8},{5,9},{6,10},{7,11},{8,12},{9,13},{1... | collective-permute-start | bytes 1474568 | tf_op jit(solution)/shard_map/ppermute | solution.py:131
  34.5 12.4 %collective-permute-start.17 = (f32[160,512]{1,0:T(8,128)S(1)}, f32[160,512]{1,0:T(8,128)S(1)}, u32[]{:S(2)}, u32[]{:S(2)}) collective-permute-start(f32[160,512]{1,0:T(8,128)S(1)} %slice.112), channel_id=1, source_target_pairs={{0,16},{1,17},{2,18},{3,19},{4,20},{5,21},{6,22},{7,23},{8,24},{9,... | collective-permute-start | bytes 983048 | tf_op jit(solution)/shard_map/ppermute | solution.py:141
  46.9 18.6 %collective-permute-start.11 = (bf16[160,1536]{1,0:T(8,128)(2,1)S(1)}, bf16[160,1536]{1,0:T(8,128)(2,1)S(1)}, u32[]{:S(2)}, u32[]{:S(2)}) collective-permute-start(bf16[160,1536]{1,0:T(8,128)(2,1)S(1)} %collective-permute-done.10), channel_id=1, source_target_pairs={{0,4},{1,5},{2,6},{3,7},{4,8},{5,9},{6,10},{7,11},{8,12},{9,13},{1... | collective-permute-start | bytes 1474568 | tf_op jit(solution)/shard_map/ppermute | solution.py:131
  47.0 18.5 %collective-permute-start.18 = (f32[160,512]{1,0:T(8,128)S(1)}, f32[160,512]{1,0:T(8,128)S(1)}, u32[]{:S(2)}, u32[]{:S(2)}) collective-permute-start(f32[160,512]{1,0:T(8,128)S(1)} %broadcast_select_fusion.16), channel_id=1, source_target_pairs={{0,4},{1,5},{2,6},{3,7},{4,8},{5,9},{6,10},{7,11},{8,12},{9,13},{1... | collective-permute-start | bytes 983048 | tf_op jit(solution)/shard_map/ppermute | solution.py:131
  47.2 28.3 %collective-permute-start.7 = (bf16[160,1536]{1,0:T(8,128)(2,1)}, bf16[160,1536]{1,0:T(8,128)(2,1)}, u32[]{:S(2)}, u32[]{:S(2)}) collective-permute-start(bf16[160,1536]{1,0:T(8,128)(2,1)} %get-tuple-element.31), channel_id=1, source_target_pairs={{0,2},{1,3},{2,0},{3,1},{4,6},{5,7},{6,4},{7,5},{8,10},{9,11},{10,... | collective-permute-start | bytes 1474568 | tf_op jit(solution)/shard_map/ppermute | solution.py:128
  65.5 9.9 %collective-permute-start.19 = (f32[160,512]{1,0:T(8,128)S(1)}, f32[160,512]{1,0:T(8,128)S(1)}, u32[]{:S(2)}, u32[]{:S(2)}) collective-permute-start(f32[160,512]{1,0:T(8,128)S(1)} %collective-permute-done.18), channel_id=1, source_target_pairs={{0,4},{1,5},{2,6},{3,7},{4,8},{5,9},{6,10},{7,11},{8,12},{9,13},{1... | collective-permute-start | bytes 983048 | tf_op jit(solution)/shard_map/ppermute | solution.py:131
  66.8 14.3 %collective-permute-start.21 = (bf16[160,1536]{1,0:T(8,128)(2,1)S(1)}, bf16[160,1536]{1,0:T(8,128)(2,1)}, u32[]{:S(2)}, u32[]{:S(2)}) collective-permute-start(bf16[160,1536]{1,0:T(8,128)(2,1)S(1)} %get-tuple-element.11), channel_id=1, source_target_pairs={{0,2},{1,3},{2,0},{3,1},{4,6},{5,7},{6,4},{7,5},{8,10},{9,11},{10,... | collective-permute-start | bytes 1474568 | tf_op jit(solution)/shard_map/ppermute | solution.py:128
  75.4 8.9 %collective-permute-start.20 = (f32[160,512]{1,0:T(8,128)S(1)}, f32[160,512]{1,0:T(8,128)S(1)}, u32[]{:S(2)}, u32[]{:S(2)}) collective-permute-start(f32[160,512]{1,0:T(8,128)S(1)} %collective-permute-done.19), channel_id=1, source_target_pairs={{0,4},{1,5},{2,6},{3,7},{4,8},{5,9},{6,10},{7,11},{8,12},{9,13},{1... | collective-permute-start | bytes 983048 | tf_op jit(solution)/shard_map/ppermute | solution.py:131
  75.4 9.1 %collective-permute-start.6 = (bf16[160,1536]{1,0:T(8,128)(2,1)}, bf16[160,1536]{1,0:T(8,128)(2,1)S(1)}, u32[]{:S(2)}, u32[]{:S(2)}) collective-permute-start(bf16[160,1536]{1,0:T(8,128)(2,1)} %get-tuple-element.31), channel_id=1, source_target_pairs={{0,1},{1,0},{2,3},{3,2},{4,5},{5,4},{6,7},{7,6},{8,9},{9,8},{10,11... | collective-permute-start | bytes 1474568 | tf_op jit(solution)/shard_map/ppermute | solution.py:128
  75.5 9.0 %collective-permute-start.8 = (bf16[160,1536]{1,0:T(8,128)(2,1)}, bf16[160,1536]{1,0:T(8,128)(2,1)S(1)}, u32[]{:S(2)}, u32[]{:S(2)}) collective-permute-start(bf16[160,1536]{1,0:T(8,128)(2,1)} %collective-permute-done.7), channel_id=1, source_target_pairs={{0,1},{1,0},{2,3},{3,2},{4,5},{5,4},{6,7},{7,6},{8,9},{9,8},{10,11... | collective-permute-start | bytes 1474568 | tf_op jit(solution)/shard_map/ppermute | solution.py:128
  81.0 7.9 %collective-permute-start.23 = (bf16[160,1536]{1,0:T(8,128)(2,1)S(1)}, bf16[160,1536]{1,0:T(8,128)(2,1)S(1)}, u32[]{:S(2)}, u32[]{:S(2)}) collective-permute-start(bf16[160,1536]{1,0:T(8,128)(2,1)S(1)} %get-tuple-element.11), channel_id=1, source_target_pairs={{0,1},{1,0},{2,3},{3,2},{4,5},{5,4},{6,7},{7,6},{8,9},{9,8},{10,11... | collective-permute-start | bytes 1474568 | tf_op jit(solution)/shard_map/ppermute | solution.py:128
  87.4 21.2 %collective-permute-start.12 = (f32[640,320]{0,1:T(8,128)S(1)}, f32[640,320]{0,1:T(8,128)S(1)}, u32[]{:S(2)}, u32[]{:S(2)}) collective-permute-start(f32[640,320]{0,1:T(8,128)S(1)} %fusion.10), channel_id=1, source_target_pairs={{0,16},{16,0},{1,17},{17,1},{2,18},{18,2},{3,19},{19,3},{4,20},{20... | collective-permute-start | bytes 2457608 | tf_op jit(solution)/shard_map/ppermute | solution.py:136
  92.0 30.7 %collective-permute-start.24 = (f32[320,512]{1,0:T(8,128)S(1)}, f32[320,512]{1,0:T(8,128)S(1)}, u32[]{:S(2)}, u32[]{:S(2)}) collective-permute-start(f32[320,512]{1,0:T(8,128)S(1)} %fusion.4), channel_id=1, source_target_pairs={{0,16},{16,0},{1,17},{17,1},{2,18},{18,2},{3,19},{19,3},{4,20},{20... | collective-permute-start | bytes 1966088 | tf_op jit(solution)/shard_map/ppermute | solution.py:136
  93.3 39.9 %collective-permute-start.28 = (f32[320,512]{1,0:T(8,128)S(1)}, f32[320,512]{1,0:T(8,128)S(1)}, u32[]{:S(2)}, u32[]{:S(2)}) collective-permute-start(f32[320,512]{1,0:T(8,128)S(1)} %fusion.9), channel_id=1, source_target_pairs={{0,16},{16,0},{1,17},{17,1},{2,18},{18,2},{3,19},{19,3},{4,20},{20... | collective-permute-start | bytes 1966088 | tf_op jit(solution)/shard_map/ppermute | solution.py:136
  111.1 24.2 %collective-permute-start.13 = (f32[160,320]{0,1:T(8,128)S(1)}, f32[160,320]{0,1:T(8,128)S(1)}, u32[]{:S(2)}, u32[]{:S(2)}) collective-permute-start(f32[160,320]{0,1:T(8,128)S(1)} %get-tuple-element.34), channel_id=1, source_target_pairs={{0,3},{1,2},{2,1},{3,0},{4,7},{5,6},{6,5},{7,4},{8,11},{9,10},{10,... | collective-permute-start | bytes 614408 | tf_op jit(solution)/shard_map/ppermute | solution.py:128
  111.2 24.7 %collective-permute-start.14 = (f32[160,320]{0,1:T(8,128)S(1)}, f32[160,320]{0,1:T(8,128)S(1)}, u32[]{:S(2)}, u32[]{:S(2)}) collective-permute-start(f32[160,320]{0,1:T(8,128)S(1)} %get-tuple-element.33), channel_id=1, source_target_pairs={{0,2},{1,3},{2,0},{3,1},{4,6},{5,7},{6,4},{7,5},{8,10},{9,11},{10,... | collective-permute-start | bytes 614408 | tf_op jit(solution)/shard_map/ppermute | solution.py:128
  111.8 24.1 %collective-permute-start.15 = (f32[160,320]{0,1:T(8,128)S(1)}, f32[160,320]{0,1:T(8,128)S(1)}, u32[]{:S(2)}, u32[]{:S(2)}) collective-permute-start(f32[160,320]{0,1:T(8,128)S(1)} %get-tuple-element.32), channel_id=1, source_target_pairs={{0,1},{1,0},{2,3},{3,2},{4,5},{5,4},{6,7},{7,6},{8,9},{9,8},{10,11... | collective-permute-start | bytes 614408 | tf_op jit(solution)/shard_map/ppermute | solution.py:128
  123.7 11.7 %collective-permute-start.25 = (f32[160,512]{1,0:T(8,128)}, f32[160,512]{1,0:T(8,128)}, u32[]{:S(2)}, u32[]{:S(2)}) collective-permute-start(f32[160,512]{1,0:T(8,128)} %slice.145), channel_id=1, source_target_pairs={{0,2},{1,3},{2,0},{3,1},{4,6},{5,7},{6,4},{7,5},{8,10},{9,11},{10,... | collective-permute-start | bytes 983048 | tf_op jit(solution)/shard_map/ppermute | solution.py:128
  134.8 13.7 %collective-permute-start.29 = (f32[320,512]{1,0:T(8,128)}, f32[320,512]{1,0:T(8,128)}, u32[]{:S(2)}, u32[]{:S(2)}) collective-permute-start(f32[320,512]{1,0:T(8,128)} %fusion.3), channel_id=1, source_target_pairs={{0,2},{1,3},{2,0},{3,1},{4,6},{5,7},{6,4},{7,5},{8,10},{9,11},{10,... | collective-permute-start | bytes 1966088 | tf_op jit(solution)/shard_map/ppermute | solution.py:128
  135.3 13.2 %collective-permute-start.27 = (f32[160,512]{1,0:T(8,128)}, f32[160,512]{1,0:T(8,128)}, u32[]{:S(2)}, u32[]{:S(2)}) collective-permute-start(f32[160,512]{1,0:T(8,128)} %slice.145), channel_id=1, source_target_pairs={{0,1},{1,0},{2,3},{3,2},{4,5},{5,4},{6,7},{7,6},{8,9},{9,8},{10,11... | collective-permute-start | bytes 983048 | tf_op jit(solution)/shard_map/ppermute | solution.py:128
  135.4 13.1 %collective-permute-start.26 = (f32[160,512]{1,0:T(8,128)}, f32[160,512]{1,0:T(8,128)}, u32[]{:S(2)}, u32[]{:S(2)}) collective-permute-start(f32[160,512]{1,0:T(8,128)} %collective-permute-done.25), channel_id=1, source_target_pairs={{0,1},{1,0},{2,3},{3,2},{4,5},{5,4},{6,7},{7,6},{8,9},{9,8},{10,11... | collective-permute-start | bytes 983048 | tf_op jit(solution)/shard_map/ppermute | solution.py:128
  138.3 47.2 %collective-permute-start.31 = (f32[320,512]{1,0:T(8,128)}, f32[320,512]{1,0:T(8,128)}, u32[]{:S(2)}, u32[]{:S(2)}) collective-permute-start(f32[320,512]{1,0:T(8,128)} %fusion.3), channel_id=1, source_target_pairs={{0,1},{1,0},{2,3},{3,2},{4,5},{5,4},{6,7},{7,6},{8,9},{9,8},{10,11... | collective-permute-start | bytes 1966088 | tf_op jit(solution)/shard_map/ppermute | solution.py:128
  148.5 37.0 %collective-permute-start.30 = (f32[320,512]{1,0:T(8,128)}, f32[320,512]{1,0:T(8,128)}, u32[]{:S(2)}, u32[]{:S(2)}) collective-permute-start(f32[320,512]{1,0:T(8,128)} %collective-permute-done.29), channel_id=1, source_target_pairs={{0,1},{1,0},{2,3},{3,2},{4,5},{5,4},{6,7},{7,6},{8,9},{9,8},{10,11... | collective-permute-start | bytes 1966088 | tf_op jit(solution)/shard_map/ppermute | solution.py:128
  (19 other events, 179.5 us)
